TPU v7x, 32 devices: a whole 2x2x4 slice. The times are simulated.
32 devices in a mesh: seq: 8 (over z, y), dp: 4 (over x, core).
Axes of the slice: x: 2, y: 2, z: 4, core: 2. Of those that a mesh axis runs over, the one named last changes fastest.
Arguments:
- inputs: float32 [4, 4096, 128], P('dp', 'seq'), may hold values from -6 to 6
- gate_values: float32 [4, 4096, 128], P('dp', 'seq'), may hold values from -6 to 6
- out_grad: float32 [4, 4096, 128], P('dp', 'seq'), may hold values from -6 to 6
- filter_taps: float32 [4096, 128], P('seq'), may hold values from -0.09375 to 0.09375
- skip_gain: float32 [128], replicated, may hold values from -4 to 4
Outputs:
- input_grad: float32 [4, 4096, 128], P('dp', 'seq')
- gate_grad: float32 [4, 4096, 128], P('dp', 'seq')
- filter_grad: float32 [4096, 128], P('seq', 'dp')
All inputs are finite; a program needn't handle non-finite values.
Results may differ from a plain program's by a relative error of at most 0.0001.
Values sent between devices are 32-bit elements; how exact they have to be, the bound alone decides.
A program may use at most 64 MiB of HBM per device.

v0:
```python
import functools
import math

import jax
import jax.numpy as jnp
import ml_dtypes
import numpy as np
from jax import lax
from jax.experimental import pallas as pl
from jax.experimental.pallas import tpu as pltpu
from jax.sharding import PartitionSpec as P

first_radix = 32


def rotation(product, modulus, direction):
    fraction = (product % modulus).astype(jnp.float32) / modulus
    turned = 2.0 * math.pi * fraction
    return (jnp.cos(turned), direction * jnp.sin(turned))


def contract(formula, matrix, operand):
    return jnp.einsum(
        formula,
        matrix,
        operand,
        precision=lax.Precision.HIGHEST,
        preferred_element_type=jnp.float32,
    )


def complex_apply(formula, table_re, table_im, values_re, values_im):
    result_re = contract(formula, table_re, values_re) - contract(formula, table_im, values_im)
    result_im = contract(formula, table_re, values_im) + contract(formula, table_im, values_re)
    return (result_re, result_im)


def local_forward(values_re, values_im):
    pairs, rows, width = values_re.shape
    second = rows // first_radix
    values_re = values_re.reshape(pairs, first_radix, second, width)
    values_im = values_im.reshape(pairs, first_radix, second, width)
    outer = jnp.arange(first_radix, dtype=jnp.int32)
    inner = jnp.arange(second, dtype=jnp.int32)
    table_re, table_im = rotation(outer[:, None] * outer[None, :], first_radix, -1.0)
    section_re, section_im = complex_apply(
        "ca,mabx->mcbx", table_re, table_im, values_re, values_im
    )
    twist_re, twist_im = rotation(outer[:, None] * inner[None, :], rows, -1.0)
    twist_re = twist_re[None, :, :, None]
    twist_im = twist_im[None, :, :, None]
    turned_re = section_re * twist_re - section_im * twist_im
    turned_im = section_re * twist_im + section_im * twist_re
    table_re, table_im = rotation(inner[:, None] * inner[None, :], second, -1.0)
    return complex_apply("db,mcbx->mcdx", table_re, table_im, turned_re, turned_im)


def local_inverse(spec_re, spec_im):
    pairs, first, second, width = spec_re.shape
    rows = first * second
    outer = jnp.arange(first, dtype=jnp.int32)
    inner = jnp.arange(second, dtype=jnp.int32)
    table_re, table_im = rotation(inner[:, None] * inner[None, :], second, 1.0)
    section_re, section_im = complex_apply("bd,mcdx->mcbx", table_re, table_im, spec_re, spec_im)
    twist_re, twist_im = rotation(outer[:, None] * inner[None, :], rows, 1.0)
    twist_re = twist_re[None, :, :, None]
    twist_im = twist_im[None, :, :, None]
    turned_re = section_re * twist_re - section_im * twist_im
    turned_im = section_re * twist_im + section_im * twist_re
    table_re, table_im = rotation(outer[:, None] * outer[None, :], first, 1.0)
    result_re, result_im = complex_apply("ac,mcbx->mabx", table_re, table_im, turned_re, turned_im)
    return (result_re.reshape(pairs, rows, width), result_im.reshape(pairs, rows, width))


def frequency_labels():
    steps = lax.axis_size("seq")
    own = lax.axis_index("seq")
    local_labels = 2 * own + jnp.arange(2, dtype=jnp.int32)
    all_labels = jnp.arange(2 * steps, dtype=jnp.int32)
    return (local_labels, all_labels)


def forward_spectrum(signal):
    rows, width = signal.shape
    steps = lax.axis_size("seq")
    piece = rows // steps
    double = 2 * steps
    total = double * rows
    columns = lax.all_to_all(
        signal.reshape(1, rows, width), "seq", split_axis=1, concat_axis=0, tiled=True
    )
    block_index = jnp.arange(steps, dtype=jnp.int32)
    freq_index = jnp.arange(double, dtype=jnp.int32)
    table_re, table_im = rotation(freq_index[:, None] * block_index[None, :], double, -1.0)
    coarse_re = contract("kq,qrc->krc", table_re, columns)
    coarse_im = contract("kq,qrc->krc", table_im, columns)
    offsets = lax.axis_index("seq") * piece + jnp.arange(piece, dtype=jnp.int32)
    twist_re, twist_im = rotation(freq_index[:, None] * offsets[None, :], total, -1.0)
    twist_re = twist_re[:, :, None]
    twist_im = twist_im[:, :, None]
    turned_re = coarse_re * twist_re - coarse_im * twist_im
    turned_im = coarse_re * twist_im + coarse_im * twist_re
    moved = lax.all_to_all(
        jnp.stack([turned_re, turned_im]), "seq", split_axis=1, concat_axis=2, tiled=True
    )
    return local_forward(moved[0], moved[1])


def inverse_time(spec_re, spec_im, local_labels, all_labels):
    pairs, first, second, width = spec_re.shape
    rows = first * second
    steps = lax.axis_size("seq")
    double = 2 * steps
    total = double * rows
    time_re, time_im = local_inverse(spec_re, spec_im)
    positions = jnp.arange(rows, dtype=jnp.int32)
    twist_re, twist_im = rotation(local_labels[:, None] * positions[None, :], total, 1.0)
    twist_re = twist_re[:, :, None]
    twist_im = twist_im[:, :, None]
    turned_re = time_re * twist_re - time_im * twist_im
    turned_im = time_re * twist_im + time_im * twist_re
    moved = lax.all_to_all(
        jnp.stack([turned_re, turned_im]), "seq", split_axis=2, concat_axis=1, tiled=True
    )
    block_index = jnp.arange(steps, dtype=jnp.int32)
    table_re, table_im = rotation(block_index[:, None] * all_labels[None, :], double, 1.0)
    result_re = (
        contract("qk,krc->qrc", table_re, moved[0]) - contract("qk,krc->qrc", table_im, moved[1])
    ) / total
    result_im = (
        contract("qk,krc->qrc", table_re, moved[1]) + contract("qk,krc->qrc", table_im, moved[0])
    ) / total
    return (result_re, result_im)


def local(inputs, gate_values, out_grad, filter_taps, skip_gain):
    seq_input = inputs[0]
    seq_gate = gate_values[0]
    seq_grad = out_grad[0]
    rows, width = seq_input.shape
    replicas = lax.axis_size("dp")
    conv_grad = seq_grad * seq_gate
    spec_re, spec_im = forward_spectrum(
        jnp.concatenate([seq_input, conv_grad, filter_taps], axis=1)
    )
    filter_re = spec_re[..., 2 * width :]
    filter_im = spec_im[..., 2 * width :]
    input_re = spec_re[..., :width]
    input_im = spec_im[..., :width]
    grad_re = spec_re[..., width : 2 * width]
    grad_im = spec_im[..., width : 2 * width]
    conv_re = filter_re * input_re - filter_im * input_im
    conv_im = filter_re * input_im + filter_im * input_re
    corr_re = filter_re * grad_re + filter_im * grad_im
    corr_im = filter_re * grad_im - filter_im * grad_re
    taps_re = input_re * grad_re + input_im * grad_im
    taps_im = input_re * grad_im - input_im * grad_re
    packed_re = conv_re - corr_im
    packed_im = conv_im + corr_re
    local_labels, all_labels = frequency_labels()
    result_re, result_im = inverse_time(
        jnp.concatenate([packed_re, taps_re], axis=3),
        jnp.concatenate([packed_im, taps_im], axis=3),
        local_labels,
        all_labels,
    )
    results = jnp.concatenate([result_re, result_im[..., :width]], axis=2)
    timeline = lax.all_to_all(results, "seq", split_axis=0, concat_axis=1, tiled=True)[0]
    conv_time = timeline[:, :width]
    corr_time = timeline[:, timeline.shape[1] - width :]
    taps_time = timeline[:, width : timeline.shape[1] - width]
    taps_time = lax.psum_scatter(taps_time, "dp", scatter_dimension=1, tiled=True)
    gate_part = seq_grad * (conv_time + skip_gain[None, :] * seq_input)
    input_part = corr_time + skip_gain[None, :] * conv_grad
    length_total = rows * lax.axis_size("seq")
    batch_total = replicas * inputs.shape[0]
    filter_part = taps_time / math.sqrt(batch_total * length_total)
    return (input_part[None], gate_part[None], filter_part)


MESH = pl.DeviceIdType.MESH


def split_halves(table):
    high = table.astype(ml_dtypes.bfloat16)
    low = (table - high.astype(np.float64)).astype(ml_dtypes.bfloat16)
    return high, low


def block_tables(rows):
    double = 2 * rows
    place = np.arange(rows)
    turned = 2.0 * np.pi * ((place[:, None] * place[None, :]) % double) / double
    real = np.cos(turned)
    imag = -np.sin(turned)
    imag[:, 0] = 1.0 - 2.0 * (place % 2)
    forward = np.concatenate([real, imag], axis=1)
    weight = np.full((double, 1), 2.0 / double)
    weight[0] = weight[rows] = 1.0 / double
    inverse = forward.T * weight
    return split_halves(forward) + split_halves(inverse)


def dot3(values, high, low):
    top = values.astype(jnp.bfloat16)
    rest = (values - top.astype(jnp.float32)).astype(jnp.bfloat16)
    dot = functools.partial(jnp.dot, preferred_element_type=jnp.float32)
    return dot(top, high) + (dot(rest, high) + dot(top, low))


def kernel(
    steps, replicas, batch_total,
    in_any, gate_any, og_any, taps_any, skip_any, fh_any, fl_any, ih_any, il_any,
    ig_any, gg_any, fg_any,
    inp, gate, og, taps, skip, fh, fl, ih, il,
    tall, tsend, trecv, xsend, xrecv, gsend, grecv,
    rows8, trows8, spec_t, spec_x, spec_g, prod, tprod,
    csend, crecv, rsend, rrecv, bsend, brecv, merged,
    load_sem, tsend_sem, trecv_sem, xsend_sem, xrecv_sem, gsend_sem, grecv_sem,
    csend_sem, crecv_sem, rsend_sem, rrecv_sem, bsend_sem, brecv_sem, store_sem,
):
    devices = steps * replicas
    pairs = replicas // 2
    own_s = lax.axis_index("seq")
    own_d = lax.axis_index("dp")
    me = own_s * replicas + own_d
    group = own_d * steps + own_s
    rows, width = inp.shape
    lanes = 128
    half = 4

    barrier = pltpu.get_barrier_semaphore()

    def greet(i, carry):
        p = lax.rem(me + i, devices)
        pl.semaphore_signal(
            barrier, inc=1, device_id=(p // replicas, lax.rem(p, replicas)), device_id_type=MESH
        )
        return carry

    loads = [
        pltpu.make_async_copy(src, dst, load_sem.at[k])
        for k, (src, dst) in enumerate([
            (taps_any, taps), (in_any, inp), (og_any, og), (gate_any, gate), (skip_any, skip),
            (fh_any, fh), (fl_any, fl), (ih_any, ih), (il_any, il),
        ])
    ]
    lax.fori_loop(1, devices, greet, 0)
    for copy in loads:
        copy.start()

    def seq_copy(src, dst, src_sem, dst_sem, s, q):
        return pltpu.make_async_remote_copy(
            src_ref=src.at[s], dst_ref=dst.at[q], send_sem=src_sem.at[s],
            recv_sem=dst_sem.at[q], device_id=(s, own_d), device_id_type=MESH,
        )

    def out_copy(src, dst, src_sem, dst_sem, p, q):
        s, d = p // replicas, lax.rem(p, replicas)
        return pltpu.make_async_remote_copy(
            src_ref=src.at[d * steps + s], dst_ref=dst.at[q // replicas, lax.rem(q, replicas)],
            send_sem=src_sem.at[p], recv_sem=dst_sem.at[q], device_id=(s, d), device_id_type=MESH,
        )

    def back_copy(src, dst, src_sem, dst_sem, p, q):
        s, d = p // replicas, lax.rem(p, replicas)
        return pltpu.make_async_remote_copy(
            src_ref=src.at[s, d], dst_ref=dst.at[lax.rem(q, replicas) * steps + q // replicas],
            send_sem=src_sem.at[p], recv_sem=dst_sem.at[q], device_id=(s, d), device_id_type=MESH,
        )

    def over_seq(use):
        def body(i, carry):
            use(lax.rem(own_s + i, steps))
            return carry

        lax.fori_loop(1, steps, body, 0)

    def over_all(use):
        def body(i, carry):
            use(lax.rem(me + stride * i, devices))
            return carry

        lax.fori_loop(1, devices, body, 0)

    t_refs = (tsend, trecv, tsend_sem, trecv_sem)
    x_refs = (xsend, xrecv, xsend_sem, xrecv_sem)
    g_refs = (gsend, grecv, gsend_sem, grecv_sem)
    c_refs = (csend, crecv, csend_sem, crecv_sem)
    r_refs = (rsend, rrecv, rsend_sem, rrecv_sem)
    b_refs = (bsend, brecv, bsend_sem, brecv_sem)

    def to_channels(values, ref):
        turned = values.T
        for k in range(width // half):
            ref[k] = turned[half * k : half * k + half]

    loads[0].wait()
    tall[...] = taps[...].T.reshape(replicas, steps * half, rows)
    mine = tall[own_d]
    for k in range(steps):
        tsend[k] = mine[half * k : half * k + half]
    loads[1].wait()
    to_channels(inp[...], xsend)
    pl.semaphore_wait(barrier, devices - 1)
    over_seq(lambda s: seq_copy(*t_refs, s, own_s).start())
    over_all(lambda p: out_copy(*x_refs, p, me).start())
    loads[2].wait()
    loads[3].wait()
    gate[...] = og[...] * gate[...]
    to_channels(gate[...], gsend)
    over_all(lambda p: out_copy(*g_refs, p, me).start())
    trecv[own_s] = tsend[own_s]
    xrecv[own_s, own_d] = xsend[group]
    grecv[own_s, own_d] = gsend[group]
    for copy in loads[4:]:
        copy.wait()

    lane = lax.broadcasted_iota(jnp.int32, (8, lanes), 1)
    sign = (1 - 2 * lax.rem(lane, 2)).astype(jnp.float32)

    def forward(ref, spec):
        for s in range(steps):
            for d in range(replicas):
                at = half * (d % 2)
                rows8[s * pairs + d // 2, at : at + half] = ref[s, d]
        spec[...] = dot3(rows8[...].reshape(steps * pairs * 8, rows), fh[...], fl[...]).reshape(
            steps, pairs, 8, 2 * rows
        )

    def backward(ref):
        result = dot3(prod[...].reshape(steps * pairs * 8, 2 * rows), ih[...], il[...])
        for s in range(steps):
            for d in range(replicas):
                at = half * (replicas * s + d)
                ref[s, d] = result[at : at + half]

    def slices(c):
        re_at = pl.ds(pl.multiple_of(c * lanes, lanes), lanes)
        im_at = pl.ds(pl.multiple_of(rows + c * lanes, lanes), lanes)
        return re_at, im_at, (lane + c * lanes) == 0

    def shifted(re, im, first):
        out_re = [re[0]] + [re[j] + sign * re[j - 1] for j in range(1, steps)]
        out_im = [im[0]] + [im[j] + sign * im[j - 1] for j in range(1, steps)]
        out_re2 = [jnp.where(first, b, a) for a, b in zip(out_re, out_im)]
        return out_re, [jnp.where(first, 0.0, b) for b in out_im], out_re2

    def add(total, term):
        return term if total is None else total + term

    def filter_blocks(re_at, im_at, first):
        return shifted(
            [spec_t[j, :, re_at] for j in range(steps)], [spec_t[j, :, im_at] for j in range(steps)], first
        )

    def blocks(spec, k, at):
        return [spec[j, k, :, at] for j in range(steps)]

    def convolve(c, carry):
        re_at, im_at, first = slices(c)
        h_re, h_im, h_re2 = filter_blocks(re_at, im_at, first)
        for k in range(pairs):
            x_re, x_im = blocks(spec_x, k, re_at), blocks(spec_x, k, im_at)
            for u in range(steps):
                re, im = None, None
                for v in range(u + 1):
                    j = u - v
                    re = add(re, h_re[j] * x_re[v] - h_im[j] * x_im[v])
                    im = add(im, h_re2[j] * x_im[v] + h_im[j] * x_re[v])
                prod[u, k, :, re_at] = re
                prod[u, k, :, im_at] = im
        return carry

    def correlate(c, carry):
        re_at, im_at, first = slices(c)
        h_re, h_im, h_re2 = filter_blocks(re_at, im_at, first)
        for k in range(pairs):
            g_re, g_im = blocks(spec_g, k, re_at), blocks(spec_g, k, im_at)
            for u in range(steps):
                re, im = None, None
                for v in range(u, steps):
                    j = v - u
                    re = add(re, h_re[j] * g_re[v] + h_im[j] * g_im[v])
                    im = add(im, h_re2[j] * g_im[v] - h_im[j] * g_re[v])
                prod[u, k, :, re_at] = re
                prod[u, k, :, im_at] = im
        return carry

    def correlate_taps(c, carry):
        re_at, im_at, first = slices(c)
        sums_re, sums_im = [None] * steps, [None] * steps
        for k in range(pairs):
            x_re, x_im, x_re2 = shifted(blocks(spec_x, k, re_at), blocks(spec_x, k, im_at), first)
            g_re, g_im = blocks(spec_g, k, re_at), blocks(spec_g, k, im_at)
            for u in range(steps):
                for v in range(u, steps):
                    j = v - u
                    sums_re[u] = add(sums_re[u], g_re[v] * x_re[j] + g_im[v] * x_im[j])
                    sums_im[u] = add(sums_im[u], g_im[v] * x_re2[j] - g_re[v] * x_im[j])
        for u in range(steps):
            tprod[u, :, re_at] = sums_re[u] + pltpu.roll(sums_re[u], half, 0)
            tprod[u, :, im_at] = sums_im[u] + pltpu.roll(sums_im[u], half, 0)
        return carry

    def to_positions(ref):
        for k in range(width // half):
            at = half * (k % 2)
            merged[k // 2, at : at + half] = ref[k]
        return merged[...].reshape(width, rows).T

    over_seq(lambda s: seq_copy(*t_refs, s, s).wait_recv())
    for k in range(steps):
        trows8[k, :half] = trecv[k]
        trows8[k, half:] = trecv[k]
    spec_t[...] = dot3(trows8[...].reshape(steps * 8, rows), fh[...], fl[...]).reshape(steps, 8, 2 * rows)

    over_all(lambda p: out_copy(*x_refs, p, p).wait_recv())
    forward(xrecv, spec_x)
    lax.fori_loop(0, rows // lanes, convolve, 0)
    backward(csend)
    over_all(lambda p: back_copy(*c_refs, p, me).start())

    over_all(lambda p: out_copy(*g_refs, p, p).wait_recv())
    forward(grecv, spec_g)
    lax.fori_loop(0, rows // lanes, correlate, 0)
    backward(rsend)
    over_all(lambda p: back_copy(*r_refs, p, me).start())

    lax.fori_loop(0, rows // lanes, correlate_taps, 0)
    folded = dot3(tprod[...].reshape(steps * 8, 2 * rows), ih[...], il[...])
    for k in range(steps):
        bsend[k] = folded[8 * k : 8 * k + half]
    over_seq(lambda s: seq_copy(*b_refs, s, own_s).start())

    crecv[group] = csend[own_s, own_d]
    rrecv[group] = rsend[own_s, own_d]
    brecv[own_s] = bsend[own_s]
    over_seq(lambda s: seq_copy(*t_refs, s, s).wait_send())
    over_all(lambda p: out_copy(*x_refs, p, p).wait_send())
    over_all(lambda p: out_copy(*g_refs, p, p).wait_send())

    over_all(lambda p: back_copy(*c_refs, p, p).wait_recv())
    gain = skip[...]
    og[...] = og[...] * (to_positions(crecv) + gain * inp[...])
    stores = [
        pltpu.make_async_copy(src, dst, store_sem.at[k])
        for k, (src, dst) in enumerate([(og, gg_any), (gate, ig_any), (tall.at[0], fg_any)])
    ]
    stores[0].start()
    over_all(lambda p: back_copy(*c_refs, p, p).wait_send())
    over_all(lambda p: back_copy(*r_refs, p, p).wait_recv())
    gate[...] = to_positions(rrecv) + gain * gate[...]
    stores[1].start()
    over_seq(lambda s: seq_copy(*b_refs, s, s).wait_recv())
    scale = 1.0 / math.sqrt(batch_total * rows * steps)
    tall[0] = scale * jnp.concatenate([brecv[k] for k in range(steps)], axis=0)
    stores[2].start()

    over_seq(lambda s: seq_copy(*b_refs, s, s).wait_send())
    over_all(lambda p: back_copy(*r_refs, p, p).wait_send())
    for copy in stores:
        copy.wait()


def hand_over(*refs):
    reads = [pltpu.make_async_copy(refs[k], refs[6 + k], refs[9].at[k]) for k in range(3)]
    writes = [pltpu.make_async_copy(refs[6 + k], refs[3 + k], refs[9].at[3 + k]) for k in range(3)]
    for copy in reads:
        copy.start()
    for read, write in zip(reads, writes):
        read.wait()
        write.start()
    for copy in writes:
        copy.wait()


stride = 1


def fused(inputs, gate_values, out_grad, filter_taps, skip_gain, steps, replicas):
    rows, width = filter_taps.shape
    devices = steps * replicas
    pairs = replicas // 2
    double = 2 * rows
    tables = block_tables(rows)
    f32, bf16 = jnp.float32, jnp.bfloat16
    dma = pltpu.SemaphoreType.DMA
    anywhere = pl.BlockSpec(memory_space=pltpu.HBM)
    block = pltpu.VMEM((rows, width), f32)
    by_seq = pltpu.VMEM((steps, 4, rows), f32)
    by_group = pltpu.VMEM((devices, 4, rows), f32)
    by_device = pltpu.VMEM((steps, replicas, 4, rows), f32)
    spectrum = pltpu.VMEM((steps, pairs, 8, double), f32)
    taps_spectrum = pltpu.VMEM((steps, 8, double), f32)
    results = pl.pallas_call(
        functools.partial(kernel, steps, replicas, replicas * inputs.shape[0]),
        out_shape=(
            jax.ShapeDtypeStruct((rows, width), f32),
            jax.ShapeDtypeStruct((rows, width), f32),
            jax.ShapeDtypeStruct((width // replicas, rows), f32),
        ),
        in_specs=[anywhere] * 9,
        out_specs=(anywhere, anywhere, anywhere),
        scratch_shapes=[block, block, block, block, pltpu.VMEM((1, width), f32)]
        + [pltpu.VMEM((rows, double), bf16)] * 2
        + [pltpu.VMEM((double, rows), bf16)] * 2
        + [pltpu.VMEM((replicas, width // replicas, rows), f32), by_seq, by_seq]
        + [by_group, by_device, by_group, by_device]
        + [pltpu.VMEM((steps * pairs, 8, rows), f32), pltpu.VMEM((steps, 8, rows), f32)]
        + [taps_spectrum, spectrum, spectrum, spectrum, taps_spectrum]
        + [by_device, by_group, by_device, by_group, by_seq, by_seq]
        + [pltpu.VMEM((width // 8, 8, rows), f32), dma((9,))]
        + [dma((n,)) for n in [steps] * 2 + [devices] * 8 + [steps] * 2 + [3]],
        compiler_params=pltpu.CompilerParams(
            collective_id=0, has_side_effects=True, vmem_limit_bytes=60 * 1024 * 1024
        ),
    )(
        inputs[0], gate_values[0], out_grad[0], filter_taps, skip_gain[None, :],
        *[jnp.asarray(table) for table in tables],
    )
    input_part, gate_part, filter_part = pl.pallas_call(
        hand_over,
        out_shape=tuple(jax.ShapeDtypeStruct(part.shape, part.dtype) for part in results),
        in_specs=[anywhere] * 3,
        out_specs=(anywhere,) * 3,
        scratch_shapes=[pltpu.VMEM(part.shape, part.dtype) for part in results] + [dma((6,))],
        compiler_params=pltpu.CompilerParams(vmem_limit_bytes=60 * 1024 * 1024),
    )(*results)
    return input_part[None], gate_part[None], filter_part.T


def solution(mesh):
    placed = (P("dp", "seq", None), P("dp", "seq", None), P("dp", "seq", None), P("seq", None), P())
    steps, replicas = mesh.shape["seq"], mesh.shape["dp"]

    def either(inputs, gate_values, out_grad, filter_taps, skip_gain):
        rows, width = filter_taps.shape
        fits = width == 4 * steps * replicas and replicas % 2 == 0 and rows % 128 == 0 and steps <= 8
        if fits and inputs.shape[0] == 1:
            return fused(inputs, gate_values, out_grad, filter_taps, skip_gain, steps, replicas)
        return local(inputs, gate_values, out_grad, filter_taps, skip_gain)

    return jax.shard_map(
        either,
        mesh=mesh,
        in_specs=placed,
        out_specs=(P("dp", "seq", None), P("dp", "seq", None), P("seq", "dp")),
        check_vma=False,
    )
```

profile of v0, /device:TPU:0, one launch (start us, length us, event | category | flops | bytes accessed | tf_op | source)
XLA Modules:
  0.0 40.7 jit_solution(16491729371720553179)
XLA Ops:
  0.6 38.3 %shard_map.112 = (f32[512,128]{1,0:T(8,128)}, f32[512,128]{1,0:T(8,128)}, f32[32,512]{1,0:T(8,128)}) custom-call(f32[512,128]{1,0:T(8,128)} %bitcast.7, f32[512,128]{1,0:T(8,128)} %bitcast.8, f32[512,128]{1,0:T(8,128)} %bitcast.9, f32[512,128]{1,0:T(8,128)} %taps_any.1, f32[1,128]{1,0:T(1,128)} %bitcast.10, bf16[512,1024]{1,0:T(8,128)(2,1)} %constant.8.clone.fh_any, ...), custom_call_target="tpu_custom_call" | custom-call | tf_op jit(solution)/shard_map/pallas_call | solution.py:496
  38.9 1.8 %shard_map.113 = (f32[512,128]{1,0:T(8,128)}, f32[512,128]{1,0:T(8,128)}, f32[32,512]{1,0:T(8,128)}) custom-call(f32[512,128]{1,0:T(8,128)} %get-tuple-element.9.refs_0_, f32[512,128]{1,0:T(8,128)} %get-tuple-element.10.refs_1_, f32[32,512]{1,0:T(8,128)} %get-tuple-element.11.refs_2_), custom_call_target="tpu_custom_call" | custom-call | tf_op jit(solution)/shard_map/pallas_call | solution.py:522
where the time goes:
time: 40.9 us; the launch traced here: 40.7 us
  Pallas kernels  40.1 us (98%)
  between operations  0.64 us (2%)
    pallas_call x1, Pallas kernels, fused(): pl.pallas_call(functools.partial(kernel, steps, replicas, replicas * inpu...  38.3 us
    pallas_call x1, Pallas kernels, fused(): pl.pallas_call(hand_over, out_shape=tuple((jax.ShapeDtypeStruct(part.shap...  1.8 us

commit v1 on v0

v1 whole, which is shorter than its diff:
```python
import functools
import math

import jax
import jax.numpy as jnp
import ml_dtypes
import numpy as np
from jax import lax
from jax.experimental import pallas as pl
from jax.experimental.pallas import tpu as pltpu
from jax.sharding import PartitionSpec as P

first_radix = 32


def rotation(product, modulus, direction):
    fraction = (product % modulus).astype(jnp.float32) / modulus
    turned = 2.0 * math.pi * fraction
    return (jnp.cos(turned), direction * jnp.sin(turned))


def contract(formula, matrix, operand):
    return jnp.einsum(
        formula,
        matrix,
        operand,
        precision=lax.Precision.HIGHEST,
        preferred_element_type=jnp.float32,
    )


def complex_apply(formula, table_re, table_im, values_re, values_im):
    result_re = contract(formula, table_re, values_re) - contract(formula, table_im, values_im)
    result_im = contract(formula, table_re, values_im) + contract(formula, table_im, values_re)
    return (result_re, result_im)


def local_forward(values_re, values_im):
    pairs, rows, width = values_re.shape
    second = rows // first_radix
    values_re = values_re.reshape(pairs, first_radix, second, width)
    values_im = values_im.reshape(pairs, first_radix, second, width)
    outer = jnp.arange(first_radix, dtype=jnp.int32)
    inner = jnp.arange(second, dtype=jnp.int32)
    table_re, table_im = rotation(outer[:, None] * outer[None, :], first_radix, -1.0)
    section_re, section_im = complex_apply(
        "ca,mabx->mcbx", table_re, table_im, values_re, values_im
    )
    twist_re, twist_im = rotation(outer[:, None] * inner[None, :], rows, -1.0)
    twist_re = twist_re[None, :, :, None]
    twist_im = twist_im[None, :, :, None]
    turned_re = section_re * twist_re - section_im * twist_im
    turned_im = section_re * twist_im + section_im * twist_re
    table_re, table_im = rotation(inner[:, None] * inner[None, :], second, -1.0)
    return complex_apply("db,mcbx->mcdx", table_re, table_im, turned_re, turned_im)


def local_inverse(spec_re, spec_im):
    pairs, first, second, width = spec_re.shape
    rows = first * second
    outer = jnp.arange(first, dtype=jnp.int32)
    inner = jnp.arange(second, dtype=jnp.int32)
    table_re, table_im = rotation(inner[:, None] * inner[None, :], second, 1.0)
    section_re, section_im = complex_apply("bd,mcdx->mcbx", table_re, table_im, spec_re, spec_im)
    twist_re, twist_im = rotation(outer[:, None] * inner[None, :], rows, 1.0)
    twist_re = twist_re[None, :, :, None]
    twist_im = twist_im[None, :, :, None]
    turned_re = section_re * twist_re - section_im * twist_im
    turned_im = section_re * twist_im + section_im * twist_re
    table_re, table_im = rotation(outer[:, None] * outer[None, :], first, 1.0)
    result_re, result_im = complex_apply("ac,mcbx->mabx", table_re, table_im, turned_re, turned_im)
    return (result_re.reshape(pairs, rows, width), result_im.reshape(pairs, rows, width))


def frequency_labels():
    steps = lax.axis_size("seq")
    own = lax.axis_index("seq")
    local_labels = 2 * own + jnp.arange(2, dtype=jnp.int32)
    all_labels = jnp.arange(2 * steps, dtype=jnp.int32)
    return (local_labels, all_labels)


def forward_spectrum(signal):
    rows, width = signal.shape
    steps = lax.axis_size("seq")
    piece = rows // steps
    double = 2 * steps
    total = double * rows
    columns = lax.all_to_all(
        signal.reshape(1, rows, width), "seq", split_axis=1, concat_axis=0, tiled=True
    )
    block_index = jnp.arange(steps, dtype=jnp.int32)
    freq_index = jnp.arange(double, dtype=jnp.int32)
    table_re, table_im = rotation(freq_index[:, None] * block_index[None, :], double, -1.0)
    coarse_re = contract("kq,qrc->krc", table_re, columns)
    coarse_im = contract("kq,qrc->krc", table_im, columns)
    offsets = lax.axis_index("seq") * piece + jnp.arange(piece, dtype=jnp.int32)
    twist_re, twist_im = rotation(freq_index[:, None] * offsets[None, :], total, -1.0)
    twist_re = twist_re[:, :, None]
    twist_im = twist_im[:, :, None]
    turned_re = coarse_re * twist_re - coarse_im * twist_im
    turned_im = coarse_re * twist_im + coarse_im * twist_re
    moved = lax.all_to_all(
        jnp.stack([turned_re, turned_im]), "seq", split_axis=1, concat_axis=2, tiled=True
    )
    return local_forward(moved[0], moved[1])


def inverse_time(spec_re, spec_im, local_labels, all_labels):
    pairs, first, second, width = spec_re.shape
    rows = first * second
    steps = lax.axis_size("seq")
    double = 2 * steps
    total = double * rows
    time_re, time_im = local_inverse(spec_re, spec_im)
    positions = jnp.arange(rows, dtype=jnp.int32)
    twist_re, twist_im = rotation(local_labels[:, None] * positions[None, :], total, 1.0)
    twist_re = twist_re[:, :, None]
    twist_im = twist_im[:, :, None]
    turned_re = time_re * twist_re - time_im * twist_im
    turned_im = time_re * twist_im + time_im * twist_re
    moved = lax.all_to_all(
        jnp.stack([turned_re, turned_im]), "seq", split_axis=2, concat_axis=1, tiled=True
    )
    block_index = jnp.arange(steps, dtype=jnp.int32)
    table_re, table_im = rotation(block_index[:, None] * all_labels[None, :], double, 1.0)
    result_re = (
        contract("qk,krc->qrc", table_re, moved[0]) - contract("qk,krc->qrc", table_im, moved[1])
    ) / total
    result_im = (
        contract("qk,krc->qrc", table_re, moved[1]) + contract("qk,krc->qrc", table_im, moved[0])
    ) / total
    return (result_re, result_im)


def local(inputs, gate_values, out_grad, filter_taps, skip_gain):
    seq_input = inputs[0]
    seq_gate = gate_values[0]
    seq_grad = out_grad[0]
    rows, width = seq_input.shape
    replicas = lax.axis_size("dp")
    conv_grad = seq_grad * seq_gate
    spec_re, spec_im = forward_spectrum(
        jnp.concatenate([seq_input, conv_grad, filter_taps], axis=1)
    )
    filter_re = spec_re[..., 2 * width :]
    filter_im = spec_im[..., 2 * width :]
    input_re = spec_re[..., :width]
    input_im = spec_im[..., :width]
    grad_re = spec_re[..., width : 2 * width]
    grad_im = spec_im[..., width : 2 * width]
    conv_re = filter_re * input_re - filter_im * input_im
    conv_im = filter_re * input_im + filter_im * input_re
    corr_re = filter_re * grad_re + filter_im * grad_im
    corr_im = filter_re * grad_im - filter_im * grad_re
    taps_re = input_re * grad_re + input_im * grad_im
    taps_im = input_re * grad_im - input_im * grad_re
    packed_re = conv_re - corr_im
    packed_im = conv_im + corr_re
    local_labels, all_labels = frequency_labels()
    result_re, result_im = inverse_time(
        jnp.concatenate([packed_re, taps_re], axis=3),
        jnp.concatenate([packed_im, taps_im], axis=3),
        local_labels,
        all_labels,
    )
    results = jnp.concatenate([result_re, result_im[..., :width]], axis=2)
    timeline = lax.all_to_all(results, "seq", split_axis=0, concat_axis=1, tiled=True)[0]
    conv_time = timeline[:, :width]
    corr_time = timeline[:, timeline.shape[1] - width :]
    taps_time = timeline[:, width : timeline.shape[1] - width]
    taps_time = lax.psum_scatter(taps_time, "dp", scatter_dimension=1, tiled=True)
    gate_part = seq_grad * (conv_time + skip_gain[None, :] * seq_input)
    input_part = corr_time + skip_gain[None, :] * conv_grad
    length_total = rows * lax.axis_size("seq")
    batch_total = replicas * inputs.shape[0]
    filter_part = taps_time / math.sqrt(batch_total * length_total)
    return (input_part[None], gate_part[None], filter_part)


MESH = pl.DeviceIdType.MESH


def split_halves(table):
    high = table.astype(ml_dtypes.bfloat16)
    low = (table - high.astype(np.float64)).astype(ml_dtypes.bfloat16)
    return high, low


def block_tables(rows):
    double = 2 * rows
    place = np.arange(rows)
    turned = 2.0 * np.pi * ((place[:, None] * place[None, :]) % double) / double
    real = np.cos(turned)
    imag = -np.sin(turned)
    imag[:, 0] = 1.0 - 2.0 * (place % 2)
    forward = np.concatenate([real, imag], axis=1)
    weight = np.full((double, 1), 2.0 / double)
    weight[0] = weight[rows] = 1.0 / double
    inverse = forward.T * weight
    return split_halves(forward) + split_halves(inverse)


def dot3(values, high, low):
    top = values.astype(jnp.bfloat16)
    rest = (values - top.astype(jnp.float32)).astype(jnp.bfloat16)
    dot = functools.partial(jnp.dot, preferred_element_type=jnp.float32)
    return dot(top, high) + (dot(rest, high) + dot(top, low))


def kernel(
    steps, replicas, batch_total,
    in_any, gate_any, og_any, taps_any, skip_any, fh_any, fl_any, ih_any, il_any,
    ig_out, gg_out, fg_out,
    inp, gate, og, taps, skip, fh, fl, ih, il,
    sig, hsend, first_in, second_in, spec_first, spec_second, filt, prod, tprod,
    out_t, out_s, out_d, res, res_cross, res_taps,
    load_sem, h_send_sem, h_recv_sem, in_send_sem, in_recv_sem, out_send_sem, out_recv_sem,
    d_send_sem, d_recv_sem,
):
    devices = steps * replicas
    own_s = lax.axis_index("seq")
    own_d = lax.axis_index("dp")
    me = own_s * replicas + own_d
    rows, width = inp.shape
    lanes = 128
    half = steps // 2
    members = half * replicas
    side = own_s // half
    other = 1 - side
    place = me - members * side
    ahead = members // 2
    inner = jnp.where(side == 0, place >= ahead, place < ahead)
    cross_first = jnp.where(side == 0, 0, ahead)
    group = lax.rem(place + ahead, members)

    barrier = pltpu.get_barrier_semaphore()

    def greet(i, carry):
        p = lax.rem(me + i, devices)
        pl.semaphore_signal(
            barrier, inc=1, device_id=(p // replicas, lax.rem(p, replicas)), device_id_type=MESH
        )
        return carry

    loads = [
        pltpu.make_async_copy(src, dst, load_sem.at[k])
        for k, (src, dst) in enumerate([
            (taps_any, taps), (in_any, inp), (og_any, og), (gate_any, gate), (skip_any, skip),
            (fh_any, fh), (fl_any, fl), (ih_any, ih), (il_any, il),
        ])
    ]
    for copy in loads:
        copy.start()
    lax.fori_loop(1, devices, greet, 0)

    def remote(src, dst, src_sem, dst_sem, s, d):
        return pltpu.make_async_remote_copy(
            src_ref=src, dst_ref=dst, send_sem=src_sem, recv_sem=dst_sem,
            device_id=(s, d), device_id_type=MESH,
        )

    def arrived(ref, sem):
        pltpu.make_async_copy(ref, ref, sem).wait()

    def repeat(low, high, use):
        def body(i, carry):
            use(i)
            return carry

        lax.fori_loop(low, high, body, 0)

    def slot_of(block, of_side):
        return jnp.where(of_side == 0, steps - 1 - block, block)

    own_row = (slot_of(own_s, side) - half) * replicas + own_d
    cross_row = slot_of(own_s, other) * replicas + own_d
    h_row = lax.rem(own_s + half, steps)

    def group_at(s):
        return lax.rem(lax.rem(s, half) * replicas + own_d + ahead, members)

    h_low = jnp.where(side == 0, 0, half // 2)
    h_high = jnp.where(side == 0, steps, half + half // 2)

    def h_copy(s, sender):
        return remote(
            hsend.at[group_at(s)], first_in.at[h_row], h_send_sem.at[s], h_recv_sem.at[side], s, own_d
        )

    def h_each(use_remote, use_local):
        def body(s):
            @pl.when(s != own_s)
            def _():
                use_remote(s)

            if use_local is not None:
                @pl.when(s == own_s)
                def _():
                    use_local()

        repeat(h_low, h_high, body)

    def own_side(kind, which, dst_ref, base):
        def body(i):
            q = lax.rem(place + i, members)
            remote(
                sig.at[which, lax.rem(q + ahead, members)], dst_ref.at[base + own_row],
                in_send_sem.at[kind], in_recv_sem.at[kind],
                half * side + q // replicas, lax.rem(q, replicas),
            ).start()

        repeat(1, members, body)
        pltpu.make_async_copy(sig.at[which, group], dst_ref.at[base + own_row], in_recv_sem.at[kind]).start()

    def crossing():
        def body(i):
            q = jnp.where(side == 0, 0, ahead) + lax.rem(lax.rem(place, ahead) + i, ahead)
            remote(
                sig.at[side, lax.rem(q + ahead, members)], second_in.at[cross_row],
                in_send_sem.at[2], in_recv_sem.at[2],
                half * other + q // replicas, lax.rem(q, replicas),
            ).start()

        repeat(0, ahead, body)

    loads[0].wait()
    hsend[...] = taps[...].T.reshape(width // 8, 8, rows)
    loads[1].wait()
    sig[0] = inp[...].T.reshape(width // 8, 8, rows)
    loads[2].wait()
    loads[3].wait()
    gate[...] = og[...] * gate[...]
    sig[1] = gate[...].T.reshape(width // 8, 8, rows)
    pl.semaphore_wait(barrier, devices - 1)

    h_each(
        lambda s: h_copy(s, s).start(),
        lambda: pltpu.make_async_copy(hsend.at[group], first_in.at[h_row], h_recv_sem.at[side]).start(),
    )
    own_side(0, side, first_in, steps)
    crossing()
    own_side(1, other, second_in, members)

    for copy in loads[4:]:
        copy.wait()

    lane = lax.broadcasted_iota(jnp.int32, (8, lanes), 1)
    sign = (1 - 2 * lax.rem(lane, 2)).astype(jnp.float32)
    turn = jnp.where(side == 0, 1.0, -1.0).astype(jnp.float32)

    def slices(c):
        re_at = pl.ds(pl.multiple_of(c * lanes, lanes), lanes)
        im_at = pl.ds(pl.multiple_of(rows + c * lanes, lanes), lanes)
        return re_at, im_at, (lane + c * lanes) == 0

    def add(total, term):
        return term if total is None else total + term

    def h_at(j):
        return (j + half) % steps

    def send_own(source, base, kind, which):
        def body(i):
            q = lax.rem(place + i, members)
            s = half * side + q // replicas
            at = (slot_of(s, side) - half) * replicas + lax.rem(q, replicas)
            remote(
                source.at[base + at], res.at[which, group], out_send_sem.at[kind], out_recv_sem.at[kind],
                s, lax.rem(q, replicas),
            ).start()

        repeat(1, members, body)
        pltpu.make_async_copy(source.at[base + own_row], res.at[which, group], out_recv_sem.at[kind]).start()

    def send_cross():
        def body(i):
            q = lax.rem(place + i, members)
            s = half * other + q // replicas
            at = slot_of(s, side) * replicas + lax.rem(q, replicas)
            remote(
                out_t.at[at], res_cross.at[lax.rem(place, ahead)], out_send_sem.at[2], out_recv_sem.at[2],
                s, lax.rem(q, replicas),
            ).start()

        repeat(0, members, body)

    d_dst = group // (members // replicas)
    d_at = lax.rem(group, members // replicas)

    def d_each(count, use_remote, use_local):
        def body(i):
            u = lax.rem(own_s + i, count)
            to_self = jnp.logical_and(u == own_s, d_dst == own_d)
            to = jnp.where(u < half, side, 0)

            @pl.when(jnp.logical_not(to_self))
            def _():
                use_remote(remote(
                    out_d.at[u], res_taps.at[to, d_at], d_send_sem.at[u], d_recv_sem, u, d_dst
                ))

            if use_local:
                @pl.when(to_self)
                def _():
                    pltpu.make_async_copy(out_d.at[u], res_taps.at[to, d_at], d_recv_sem).start()

        repeat(0, count, body)

    def work(low):
        count = steps - low
        arrived(first_in.at[pl.ds(half, half)], h_recv_sem.at[0])
        if low == 0:
            arrived(first_in.at[pl.ds(0, half)], h_recv_sem.at[1])
        arrived(first_in.at[pl.ds(steps, members)], in_recv_sem.at[0])
        size = steps + members - low
        spec_first[pl.ds(low, size)] = dot3(
            first_in[pl.ds(low, size)].reshape(size * 8, rows), fh[...], fl[...]
        ).reshape(size, 8, 2 * rows)

        def prepare(c):
            re_at, im_at, first = slices(c)
            re = [spec_first[h_at(j), :, re_at] for j in range(count)]
            im = [spec_first[h_at(j), :, im_at] for j in range(count)]
            for j in range(count):
                out_re = re[j] if j == 0 else re[j] + sign * re[j - 1]
                out_im = im[j] if j == 0 else im[j] + sign * im[j - 1]
                filt[0, j, :, re_at] = out_re
                filt[1, j, :, re_at] = jnp.where(first, 0.0, turn * out_im)
                filt[2, j, :, re_at] = jnp.where(first, out_im, out_re)

        repeat(0, rows // lanes, prepare)

        def filters(re_at):
            return [[filt[i, j, :, re_at] for j in range(count)] for i in range(3)]

        def first_products(i):
            c, k = i // replicas, lax.rem(i, replicas)
            re_at, im_at, _ = slices(c)
            h_re, h_im, h_re2 = filters(re_at)
            t_re = [spec_first[steps + v * replicas + k, :, re_at] for v in range(half)]
            t_im = [spec_first[steps + v * replicas + k, :, im_at] for v in range(half)]
            for u in range(low, steps):
                re, im = None, None
                for v in range(max(u, half), steps):
                    j, w = v - u, v - half
                    re = add(re, h_re[j] * t_re[w] - h_im[j] * t_im[w])
                    im = add(im, h_re2[j] * t_im[w] + h_im[j] * t_re[w])
                prod[u * replicas + k, :, re_at] = re
                prod[u * replicas + k, :, im_at] = im

        repeat(0, rows // lanes * replicas, first_products)

        def inverse(source, start, size):
            return dot3(
                source[pl.ds(start, size)].reshape(size * 8, 2 * rows), ih[...], il[...]
            ).reshape(size, 8, rows)

        if low == 0:
            out_t[pl.ds(0, members)] = inverse(prod, 0, members)
            send_cross()
        out_t[pl.ds(members, members)] = inverse(prod, members, members)
        send_own(out_t, members, 0, side)

        arrived(second_in.at[pl.ds(members, members)], in_recv_sem.at[1])
        if low == 0:
            arrived(second_in.at[pl.ds(0, members)], in_recv_sem.at[2])
        start, size = low * replicas, count * replicas
        spec_second[pl.ds(start, size)] = dot3(
            second_in[pl.ds(start, size)].reshape(size * 8, rows), fh[...], fl[...]
        ).reshape(size, 8, 2 * rows)

        def second_products(i):
            c, k = i // replicas, lax.rem(i, replicas)
            re_at, im_at, _ = slices(c)
            h_re, h_im, h_re2 = filters(re_at)
            s_re = [spec_second[v * replicas + k, :, re_at] for v in range(low, steps)]
            s_im = [spec_second[v * replicas + k, :, im_at] for v in range(low, steps)]
            for u in range(half, steps):
                re, im = None, None
                for v in range(low, u + 1):
                    j, w = u - v, v - low
                    re = add(re, h_re[j] * s_re[w] + h_im[j] * s_im[w])
                    im = add(im, h_re2[j] * s_im[w] - h_im[j] * s_re[w])
                prod[(u - half) * replicas + k, :, re_at] = re
                prod[(u - half) * replicas + k, :, im_at] = im

        repeat(0, rows // lanes * replicas, second_products)
        out_s[...] = inverse(prod, 0, members)
        send_own(out_s, 0, 1, other)

        def taps_products(c):
            re_at, im_at, first = slices(c)
            flip = jnp.where(first, 1.0, -turn)
            sums_re, sums_im = [None] * count, [None] * count
            for k in range(replicas):
                t_re = [spec_first[steps + v * replicas + k, :, re_at] for v in range(half)]
                t_im = [spec_first[steps + v * replicas + k, :, im_at] for v in range(half)]
                for s in range(low, steps):
                    s_re = spec_second[s * replicas + k, :, re_at]
                    s_im = spec_second[s * replicas + k, :, im_at]
                    s_re2 = jnp.where(first, s_im, s_re)
                    s_im = jnp.where(first, 0.0, s_im)
                    for v in range(max(s, half), steps):
                        m, w = v - s, v - half
                        sums_re[m] = add(sums_re[m], t_re[w] * s_re + t_im[w] * s_im)
                        sums_im[m] = add(sums_im[m], t_im[w] * s_re2 - t_re[w] * s_im)
            for m in range(count):
                last = m == count - 1
                tprod[m, :, re_at] = sums_re[m] if last else sums_re[m] + sign * sums_re[m + 1]
                tprod[m, :, im_at] = flip * (sums_im[m] if last else sums_im[m] + sign * sums_im[m + 1])

        repeat(0, rows // lanes, taps_products)
        out_d[pl.ds(0, count)] = inverse(tprod, 0, count)
        d_each(count, lambda copy: copy.start(), True)

    pl.when(inner)(lambda: work(0))
    pl.when(jnp.logical_not(inner))(lambda: work(half))

    gain = skip[...]

    def positions(which):
        return res[which].reshape(width, rows).T

    def finish(is_second):
        ranges = pl.ds(0, ahead) if is_second else pl.ds(ahead, ahead)
        arrived(res.at[1 if is_second else 0], out_recv_sem.at[0])
        if is_second:
            ig_out[...] = positions(1) + gain * gate[...]
        else:
            gg_out[...] = og[...] * (positions(0) + gain * inp[...])
        late = 0 if is_second else 1
        arrived(res_cross, out_recv_sem.at[2])
        arrived(res.at[late], out_recv_sem.at[1])
        res[late, ranges] = res[late, ranges] + res_cross[...]
        if is_second:
            gg_out[...] = og[...] * (positions(0) + gain * inp[...])
        else:
            ig_out[...] = positions(1) + gain * gate[...]
        scale = 1.0 / math.sqrt(batch_total * rows * steps)
        if is_second:
            arrived(res_taps.at[0], d_recv_sem)
            total = res_taps[0]
        else:
            arrived(res_taps, d_recv_sem)
            total = res_taps[0] + res_taps[1]
        fg_out[...] = scale * total.reshape(width // replicas, rows)

    pl.when(side == 0)(lambda: finish(False))
    pl.when(side == 1)(lambda: finish(True))

    h_each(lambda s: h_copy(s, s).wait_send(), None)
    arrived(sig.at[0, pl.ds(0, members - 1)], in_send_sem.at[0])
    arrived(sig.at[0, pl.ds(0, members - 1)], in_send_sem.at[1])
    arrived(sig.at[0, pl.ds(0, ahead)], in_send_sem.at[2])
    arrived(sig.at[0, pl.ds(0, members - 1)], out_send_sem.at[0])
    arrived(sig.at[0, pl.ds(0, members - 1)], out_send_sem.at[1])

    @pl.when(inner)
    def _():
        arrived(sig.at[0], out_send_sem.at[2])
        d_each(steps, lambda copy: copy.wait_send(), False)

    @pl.when(jnp.logical_not(inner))
    def _():
        d_each(half, lambda copy: copy.wait_send(), False)


def hand_over(*refs):
    writes = [pltpu.make_async_copy(refs[k], refs[3 + k], refs[6].at[k]) for k in range(3)]
    for copy in writes:
        copy.start()
    for copy in writes:
        copy.wait()


def fused(inputs, gate_values, out_grad, filter_taps, skip_gain, steps, replicas):
    rows, width = filter_taps.shape
    double = 2 * rows
    members = steps * replicas // 2
    tables = block_tables(rows)
    f32, bf16 = jnp.float32, jnp.bfloat16
    dma = pltpu.SemaphoreType.DMA
    anywhere = pl.BlockSpec(memory_space=pltpu.HBM)
    near = pl.BlockSpec(memory_space=pltpu.VMEM)
    block = pltpu.VMEM((rows, width), f32)

    def tiles(*shape):
        return pltpu.VMEM(shape + (8, rows), f32)

    def spectra(count):
        return pltpu.VMEM((count, 8, double), f32)

    results = pl.pallas_call(
        functools.partial(kernel, steps, replicas, replicas * inputs.shape[0]),
        out_shape=(
            pltpu.VMEM((rows, width), f32),
            pltpu.VMEM((rows, width), f32),
            pltpu.VMEM((width // replicas, rows), f32),
        ),
        in_specs=[anywhere] * 9,
        out_specs=(near, near, near),
        scratch_shapes=[block, block, block, block, pltpu.VMEM((1, width), f32)]
        + [pltpu.VMEM((rows, double), bf16)] * 2
        + [pltpu.VMEM((double, rows), bf16)] * 2
        + [tiles(2, width // 8), tiles(width // 8), tiles(steps + members), tiles(2 * members)]
        + [spectra(steps + members), spectra(2 * members), tiles(3, steps)]
        + [spectra(2 * members), spectra(steps)]
        + [tiles(2 * members), tiles(members), tiles(steps)]
        + [tiles(2, width // 8), tiles(width // 16), tiles(2, width // 8 // replicas)]
        + [dma((9,)), dma((steps,)), dma((2,)), dma((3,)), dma((3,)), dma((3,)), dma((3,)), dma((steps,)), dma]
        ,
        compiler_params=pltpu.CompilerParams(
            collective_id=0, has_side_effects=True, vmem_limit_bytes=48 * 1024 * 1024
        ),
    )(
        *[
            pltpu.with_memory_space_constraint(value, pltpu.HBM)
            for value in (
                inputs[0], gate_values[0], out_grad[0], filter_taps, skip_gain[None, :],
                *[jnp.asarray(table) for table in tables],
            )
        ],
    )
    input_part, gate_part, filter_part = pl.pallas_call(
        hand_over,
        out_shape=tuple(jax.ShapeDtypeStruct(part.shape, part.dtype) for part in results),
        in_specs=[near] * 3,
        out_specs=(anywhere,) * 3,
        scratch_shapes=[dma((3,))],
        compiler_params=pltpu.CompilerParams(vmem_limit_bytes=2 * 1024 * 1024),
    )(*results)
    return input_part[None], gate_part[None], filter_part.T


def solution(mesh):
    placed = (P("dp", "seq", None), P("dp", "seq", None), P("dp", "seq", None), P("seq", None), P())
    steps, replicas = mesh.shape["seq"], mesh.shape["dp"]

    def either(inputs, gate_values, out_grad, filter_taps, skip_gain):
        rows, width = filter_taps.shape
        fits = width == 128 and (steps, replicas) == (8, 4) and rows % 128 == 0
        if fits and inputs.shape[0] == 1:
            return fused(inputs, gate_values, out_grad, filter_taps, skip_gain, steps, replicas)
        return local(inputs, gate_values, out_grad, filter_taps, skip_gain)

    return jax.shard_map(
        either,
        mesh=mesh,
        in_specs=placed,
        out_specs=(P("dp", "seq", None), P("dp", "seq", None), P("seq", "dp")),
        check_vma=False,
    )
```

time: 40.9 us -> 32.8 us (0.80)
  Pallas kernels: 40.1 us -> 31.7 us
    pallas_call x1, Pallas kernels: 38.3 us -> 30.9 us  [fused(): pl.pallas_call(functools.partial(kernel, steps, replicas, replicas * inpu...]
    pallas_call x1, Pallas kernels: 1.8 us -> 0.83 us  [fused(): pl.pallas_call(hand_over, out_shape=tuple((jax.ShapeDtypeStruct(part.shap...]
where the time goes in v1:
time: 32.8 us; the launch traced here: 32.3 us
  Pallas kernels  31.7 us (97%)
  between operations  0.64 us (2%)
    pallas_call x1, Pallas kernels, fused(): pl.pallas_call(functools.partial(kernel, steps, replicas, replicas * inpu...  30.9 us
    pallas_call x1, Pallas kernels, fused(): pl.pallas_call(hand_over, out_shape=tuple((jax.ShapeDtypeStruct(part.shap...  0.83 us

profile of v1, /device:TPU:0, one launch (start us, length us, event | category | flops | bytes accessed | tf_op | source)
XLA Modules:
  0.0 32.3 jit_solution(4643845129577548446)
XLA Ops:
  0.6 30.9 %shard_map.112 = (f32[512,128]{1,0:T(8,128)S(1)}, f32[512,128]{1,0:T(8,128)S(1)}, f32[32,512]{1,0:T(8,128)S(1)}) custom-call(f32[512,128]{1,0:T(8,128)} %bitcast.7, f32[512,128]{1,0:T(8,128)} %bitcast.8, f32[512,128]{1,0:T(8,128)} %bitcast.9, f32[512,128]{1,0:T(8,128)} %taps_any.1, f32[1,128]{1,0:T(1,128)} %bitcast.10, ...), custom_call_target="tpu_custom_call" | custom-call | tf_op jit(solution)/shard_map/pallas_call | solution.py:594
  31.5 0.8 %shard_map.113 = (f32[512,128]{1,0:T(8,128)}, f32[512,128]{1,0:T(8,128)}, f32[32,512]{1,0:T(8,128)}) custom-call(f32[512,128]{1,0:T(8,128)S(1)} %get-tuple-element.9.refs_0_, f32[512,128]{1,0:T(8,128)S(1)} %get-tuple-element.10.refs_1_, f32[32,512]{1,0:T(8,128)S(1)} %get-tuple-element.11.refs_2_), custom_call_target="tpu_custom_call" | custom-call | tf_op jit(solution)/shard_map/pallas_call | solution.py:625

commit v2 on v1

--- a/solution.py
+++ b/solution.py
@@ -214,7 +214,7 @@
     ig_out, gg_out, fg_out,
     inp, gate, og, taps, skip, fh, fl, ih, il,
     sig, hsend, first_in, second_in, spec_first, spec_second, filt, prod, tprod,
-    out_t, out_s, out_d, res, res_cross, res_taps,
+    out_t, out_s, out_d, res, res_cross, res_taps, part,
     load_sem, h_send_sem, h_recv_sem, in_send_sem, in_recv_sem, out_send_sem, out_recv_sem,
     d_send_sem, d_recv_sem,
 ):
@@ -324,22 +324,29 @@
 
         repeat(0, ahead, body)
 
+    def prepare_input():
+        loads[1].wait()
+        sig[0] = inp[...].T.reshape(width // 8, 8, rows)
+
+    def prepare_grad():
+        loads[2].wait()
+        loads[3].wait()
+        gate[...] = og[...] * gate[...]
+        sig[1] = gate[...].T.reshape(width // 8, 8, rows)
+
     loads[0].wait()
     hsend[...] = taps[...].T.reshape(width // 8, 8, rows)
-    loads[1].wait()
-    sig[0] = inp[...].T.reshape(width // 8, 8, rows)
-    loads[2].wait()
-    loads[3].wait()
-    gate[...] = og[...] * gate[...]
-    sig[1] = gate[...].T.reshape(width // 8, 8, rows)
+    pl.when(side == 0)(prepare_input)
+    pl.when(side == 1)(prepare_grad)
     pl.semaphore_wait(barrier, devices - 1)
-
     h_each(
         lambda s: h_copy(s, s).start(),
         lambda: pltpu.make_async_copy(hsend.at[group], first_in.at[h_row], h_recv_sem.at[side]).start(),
     )
     own_side(0, side, first_in, steps)
     crossing()
+    pl.when(side == 0)(prepare_grad)
+    pl.when(side == 1)(prepare_input)
     own_side(1, other, second_in, members)
 
     for copy in loads[4:]:
@@ -388,35 +395,41 @@
     d_dst = group // (members // replicas)
     d_at = lax.rem(group, members // replicas)
 
-    def d_each(count, use_remote, use_local):
+    def d_each(use_remote, use_local):
         def body(i):
-            u = lax.rem(own_s + i, count)
+            u = lax.rem(own_s + i, steps)
             to_self = jnp.logical_and(u == own_s, d_dst == own_d)
-            to = jnp.where(u < half, side, 0)
 
             @pl.when(jnp.logical_not(to_self))
             def _():
                 use_remote(remote(
-                    out_d.at[u], res_taps.at[to, d_at], d_send_sem.at[u], d_recv_sem, u, d_dst
+                    out_d.at[u], res_taps.at[d_at], d_send_sem.at[u], d_recv_sem.at[0], u, d_dst
                 ))
 
             if use_local:
                 @pl.when(to_self)
                 def _():
-                    pltpu.make_async_copy(out_d.at[u], res_taps.at[to, d_at], d_recv_sem).start()
-
-        repeat(0, count, body)
+                    pltpu.make_async_copy(out_d.at[u], res_taps.at[d_at], d_recv_sem.at[0]).start()
+
+        repeat(0, steps, body)
+
+    def part_copy():
+        return remote(
+            out_d.at[pl.ds(0, half)], part, d_send_sem.at[0], d_recv_sem.at[1],
+            lax.rem(own_s + half, steps), own_d,
+        )
 
     def work(low):
         count = steps - low
+        def transform_first(start, size):
+            spec_first[pl.ds(start, size)] = dot3(
+                first_in[pl.ds(start, size)].reshape(size * 8, rows), fh[...], fl[...]
+            ).reshape(size, 8, 2 * rows)
+
         arrived(first_in.at[pl.ds(half, half)], h_recv_sem.at[0])
         if low == 0:
             arrived(first_in.at[pl.ds(0, half)], h_recv_sem.at[1])
-        arrived(first_in.at[pl.ds(steps, members)], in_recv_sem.at[0])
-        size = steps + members - low
-        spec_first[pl.ds(low, size)] = dot3(
-            first_in[pl.ds(low, size)].reshape(size * 8, rows), fh[...], fl[...]
-        ).reshape(size, 8, 2 * rows)
+        transform_first(low, count)
 
         def prepare(c):
             re_at, im_at, first = slices(c)
@@ -430,6 +443,8 @@
                 filt[2, j, :, re_at] = jnp.where(first, out_im, out_re)
 
         repeat(0, rows // lanes, prepare)
+        arrived(first_in.at[pl.ds(steps, members)], in_recv_sem.at[0])
+        transform_first(steps, members)
 
         def filters(re_at):
             return [[filt[i, j, :, re_at] for j in range(count)] for i in range(3)]
@@ -462,13 +477,16 @@
         out_t[pl.ds(members, members)] = inverse(prod, members, members)
         send_own(out_t, members, 0, side)
 
-        arrived(second_in.at[pl.ds(members, members)], in_recv_sem.at[1])
+        def transform(start):
+            spec_second[pl.ds(start, members)] = dot3(
+                second_in[pl.ds(start, members)].reshape(members * 8, rows), fh[...], fl[...]
+            ).reshape(members, 8, 2 * rows)
+
         if low == 0:
             arrived(second_in.at[pl.ds(0, members)], in_recv_sem.at[2])
-        start, size = low * replicas, count * replicas
-        spec_second[pl.ds(start, size)] = dot3(
-            second_in[pl.ds(start, size)].reshape(size * 8, rows), fh[...], fl[...]
-        ).reshape(size, 8, 2 * rows)
+            transform(0)
+        arrived(second_in.at[pl.ds(members, members)], in_recv_sem.at[1])
+        transform(members)
 
         def second_products(i):
             c, k = i // replicas, lax.rem(i, replicas)
@@ -484,10 +502,6 @@
                     im = add(im, h_re2[j] * s_im[w] - h_im[j] * s_re[w])
                 prod[(u - half) * replicas + k, :, re_at] = re
                 prod[(u - half) * replicas + k, :, im_at] = im
-
-        repeat(0, rows // lanes * replicas, second_products)
-        out_s[...] = inverse(prod, 0, members)
-        send_own(out_s, 0, 1, other)
 
         def taps_products(c):
             re_at, im_at, first = slices(c)
@@ -510,9 +524,27 @@
                 tprod[m, :, re_at] = sums_re[m] if last else sums_re[m] + sign * sums_re[m + 1]
                 tprod[m, :, im_at] = flip * (sums_im[m] if last else sums_im[m] + sign * sums_im[m + 1])
 
-        repeat(0, rows // lanes, taps_products)
-        out_d[pl.ds(0, count)] = inverse(tprod, 0, count)
-        d_each(count, lambda copy: copy.start(), True)
+        def finish_second():
+            repeat(0, rows // lanes * replicas, second_products)
+            out_s[...] = inverse(prod, 0, members)
+            send_own(out_s, 0, 1, other)
+
+        def finish_taps():
+            repeat(0, rows // lanes, taps_products)
+            out_d[pl.ds(0, count)] = inverse(tprod, 0, count)
+            if low == 0:
+                arrived(part, d_recv_sem.at[1])
+                out_d[pl.ds(0, half)] = out_d[pl.ds(0, half)] + part[...]
+                d_each(lambda copy: copy.start(), True)
+            else:
+                part_copy().start()
+
+        if low == 0:
+            finish_second()
+            finish_taps()
+        else:
+            finish_taps()
+            finish_second()
 
     pl.when(inner)(lambda: work(0))
     pl.when(jnp.logical_not(inner))(lambda: work(half))
@@ -538,13 +570,8 @@
         else:
             ig_out[...] = positions(1) + gain * gate[...]
         scale = 1.0 / math.sqrt(batch_total * rows * steps)
-        if is_second:
-            arrived(res_taps.at[0], d_recv_sem)
-            total = res_taps[0]
-        else:
-            arrived(res_taps, d_recv_sem)
-            total = res_taps[0] + res_taps[1]
-        fg_out[...] = scale * total.reshape(width // replicas, rows)
+        arrived(res_taps, d_recv_sem.at[0])
+        fg_out[...] = scale * res_taps[...].reshape(width // replicas, rows)
 
     pl.when(side == 0)(lambda: finish(False))
     pl.when(side == 1)(lambda: finish(True))
@@ -559,11 +586,11 @@
     @pl.when(inner)
     def _():
         arrived(sig.at[0], out_send_sem.at[2])
-        d_each(steps, lambda copy: copy.wait_send(), False)
+        d_each(lambda copy: copy.wait_send(), False)
 
     @pl.when(jnp.logical_not(inner))
     def _():
-        d_each(half, lambda copy: copy.wait_send(), False)
+        part_copy().wait_send()
 
 
 def hand_over(*refs):
@@ -607,9 +634,8 @@
         + [spectra(steps + members), spectra(2 * members), tiles(3, steps)]
         + [spectra(2 * members), spectra(steps)]
         + [tiles(2 * members), tiles(members), tiles(steps)]
-        + [tiles(2, width // 8), tiles(width // 16), tiles(2, width // 8 // replicas)]
-        + [dma((9,)), dma((steps,)), dma((2,)), dma((3,)), dma((3,)), dma((3,)), dma((3,)), dma((steps,)), dma]
-        ,
+        + [tiles(2, width // 8), tiles(width // 16), tiles(width // 8 // replicas), tiles(steps // 2)]
+        + [dma((9,)), dma((steps,)), dma((2,)), dma((3,)), dma((3,)), dma((3,)), dma((3,)), dma((steps,)), dma((2,))],
         compiler_params=pltpu.CompilerParams(
             collective_id=0, has_side_effects=True, vmem_limit_bytes=48 * 1024 * 1024
         ),

time: 32.8 us -> 31.7 us (0.966)
  Pallas kernels: 31.7 us -> 30.6 us
    pallas_call x1, Pallas kernels: 30.9 us -> 29.8 us  [fused(): pl.pallas_call(functools.partial(kernel, steps, replicas, replicas * inpu...]
where the time goes in v2:
time: 31.7 us; the launch traced here: 31.3 us
  Pallas kernels  30.6 us (97%)
  between operations  0.64 us (2%)
    pallas_call x1, Pallas kernels, fused(): pl.pallas_call(functools.partial(kernel, steps, replicas, replicas * inpu...  29.8 us
    pallas_call x1, Pallas kernels, fused(): pl.pallas_call(hand_over, out_shape=tuple((jax.ShapeDtypeStruct(part.shap...  0.83 us

profile of v2, /device:TPU:0, one launch (start us, length us, event | category | flops | bytes accessed | tf_op | source)
XLA Modules:
  0.0 31.3 jit_solution(13311273432142763709)
XLA Ops:
  0.6 29.8 %shard_map.112 = (f32[512,128]{1,0:T(8,128)S(1)}, f32[512,128]{1,0:T(8,128)S(1)}, f32[32,512]{1,0:T(8,128)S(1)}) custom-call(f32[512,128]{1,0:T(8,128)} %bitcast.7, f32[512,128]{1,0:T(8,128)} %bitcast.8, f32[512,128]{1,0:T(8,128)} %bitcast.9, f32[512,128]{1,0:T(8,128)} %taps_any.1, f32[1,128]{1,0:T(1,128)} %bitcast.10, ...), custom_call_target="tpu_custom_call" | custom-call | tf_op jit(solution)/shard_map/pallas_call | solution.py:621
  30.5 0.8 %shard_map.113 = (f32[512,128]{1,0:T(8,128)}, f32[512,128]{1,0:T(8,128)}, f32[32,512]{1,0:T(8,128)}) custom-call(f32[512,128]{1,0:T(8,128)S(1)} %get-tuple-element.9.refs_0_, f32[512,128]{1,0:T(8,128)S(1)} %get-tuple-element.10.refs_1_, f32[32,512]{1,0:T(8,128)S(1)} %get-tuple-element.11.refs_2_), custom_call_target="tpu_custom_call" | custom-call | tf_op jit(solution)/shard_map/pallas_call | solution.py:651

commit v3 on v2

--- a/solution.py
+++ b/solution.py
@@ -205,7 +205,9 @@
     top = values.astype(jnp.bfloat16)
     rest = (values - top.astype(jnp.float32)).astype(jnp.bfloat16)
     dot = functools.partial(jnp.dot, preferred_element_type=jnp.float32)
-    return dot(top, high) + (dot(rest, high) + dot(top, low))
+    both = dot(jnp.concatenate([top, rest], axis=0), high)
+    count = values.shape[0]
+    return both[:count] + (both[count:] + dot(top, low))
 
 
 def kernel(
@@ -367,9 +369,19 @@
     def h_at(j):
         return (j + half) % steps
 
-    def send_own(source, base, kind, which):
+    def first_served(use):
         def body(i):
             q = lax.rem(place + i, members)
+            pl.when(jnp.logical_and(q >= 4, q != place))(lambda: use(q))
+
+        def served(q):
+            pl.when(q != place)(lambda: use(q))
+
+        repeat(0, 4, served)
+        repeat(1, members, body)
+
+    def send_own(source, base, kind, which):
+        def use(q):
             s = half * side + q // replicas
             at = (slot_of(s, side) - half) * replicas + lax.rem(q, replicas)
             remote(
@@ -377,12 +389,11 @@
                 s, lax.rem(q, replicas),
             ).start()
 
-        repeat(1, members, body)
+        first_served(use)
         pltpu.make_async_copy(source.at[base + own_row], res.at[which, group], out_recv_sem.at[kind]).start()
 
     def send_cross():
-        def body(i):
-            q = lax.rem(place + i, members)
+        def use(q):
             s = half * other + q // replicas
             at = slot_of(s, side) * replicas + lax.rem(q, replicas)
             remote(
@@ -390,14 +401,15 @@
                 s, lax.rem(q, replicas),
             ).start()
 
-        repeat(0, members, body)
+        repeat(0, 4, use)
+        repeat(0, members, lambda i: pl.when(lax.rem(place + i, members) >= 4)(lambda: use(lax.rem(place + i, members))))
 
     d_dst = group // (members // replicas)
     d_at = lax.rem(group, members // replicas)
 
-    def d_each(use_remote, use_local):
+    def d_each(start, use_remote, use_local):
         def body(i):
-            u = lax.rem(own_s + i, steps)
+            u = start + i
             to_self = jnp.logical_and(u == own_s, d_dst == own_d)
 
             @pl.when(jnp.logical_not(to_self))
@@ -411,7 +423,7 @@
                 def _():
                     pltpu.make_async_copy(out_d.at[u], res_taps.at[d_at], d_recv_sem.at[0]).start()
 
-        repeat(0, steps, body)
+        repeat(0, half, body)
 
     def part_copy():
         return remote(
@@ -482,66 +494,82 @@
                 second_in[pl.ds(start, members)].reshape(members * 8, rows), fh[...], fl[...]
             ).reshape(members, 8, 2 * rows)
 
+        def second_products(begin, end, extend):
+            def body(i):
+                c, k = i // replicas, lax.rem(i, replicas)
+                re_at, im_at, _ = slices(c)
+                h_re, h_im, h_re2 = filters(re_at)
+                s_re = [spec_second[v * replicas + k, :, re_at] for v in range(begin, end)]
+                s_im = [spec_second[v * replicas + k, :, im_at] for v in range(begin, end)]
+                for u in range(half, steps):
+                    at = (u - half) * replicas + k
+                    re, im = (prod[at, :, re_at], prod[at, :, im_at]) if extend else (None, None)
+                    for v in range(begin, min(u + 1, end)):
+                        j, w = u - v, v - begin
+                        re = add(re, h_re[j] * s_re[w] + h_im[j] * s_im[w])
+                        im = add(im, h_re2[j] * s_im[w] - h_im[j] * s_re[w])
+                    prod[at, :, re_at] = re
+                    prod[at, :, im_at] = im
+
+            repeat(0, rows // lanes * replicas, body)
+
+        def taps_products(begin, end, extend):
+            def body(c):
+                re_at, im_at, first = slices(c)
+                flip = jnp.where(first, 1.0, -turn)
+                sums_re, sums_im = [None] * (steps + 1), [None] * (steps + 1)
+                for k in range(replicas):
+                    t_re = [spec_first[steps + v * replicas + k, :, re_at] for v in range(half)]
+                    t_im = [spec_first[steps + v * replicas + k, :, im_at] for v in range(half)]
+                    for s in range(begin, end):
+                        s_re = spec_second[s * replicas + k, :, re_at]
+                        s_im = spec_second[s * replicas + k, :, im_at]
+                        s_re2 = jnp.where(first, s_im, s_re)
+                        s_im = jnp.where(first, 0.0, s_im)
+                        for v in range(max(s, half), steps):
+                            m, w = v - s, v - half
+                            sums_re[m] = add(sums_re[m], t_re[w] * s_re + t_im[w] * s_im)
+                            sums_im[m] = add(sums_im[m], t_im[w] * s_re2 - t_re[w] * s_im)
+
+                def folded(sums, m):
+                    if sums[m] is None:
+                        return sign * sums[m + 1]
+                    return sums[m] if sums[m + 1] is None else sums[m] + sign * sums[m + 1]
+
+                for m in range(half if end == steps else steps):
+                    re, im = folded(sums_re, m), flip * folded(sums_im, m)
+                    tprod[m, :, re_at] = tprod[m, :, re_at] + re if extend else re
+                    tprod[m, :, im_at] = tprod[m, :, im_at] + im if extend else im
+
+            repeat(0, rows // lanes, body)
+
+        def finish_second():
+            second_products(half, steps, low == 0)
+            out_s[...] = inverse(prod, 0, members)
+            send_own(out_s, 0, 1, other)
+
+        def finish_taps():
+            taps_products(half, steps, low == 0)
+            out_d[pl.ds(0, half)] = inverse(tprod, 0, half)
+            if low == 0:
+                arrived(part, d_recv_sem.at[1])
+                out_d[pl.ds(0, half)] = out_d[pl.ds(0, half)] + part[...]
+                d_each(0, lambda copy: copy.start(), True)
+            else:
+                part_copy().start()
+
         if low == 0:
             arrived(second_in.at[pl.ds(0, members)], in_recv_sem.at[2])
             transform(0)
+            taps_products(0, half, False)
+            out_d[pl.ds(half, half)] = inverse(tprod, half, half)
+            d_each(half, lambda copy: copy.start(), True)
+            second_products(0, half, False)
         arrived(second_in.at[pl.ds(members, members)], in_recv_sem.at[1])
         transform(members)
-
-        def second_products(i):
-            c, k = i // replicas, lax.rem(i, replicas)
-            re_at, im_at, _ = slices(c)
-            h_re, h_im, h_re2 = filters(re_at)
-            s_re = [spec_second[v * replicas + k, :, re_at] for v in range(low, steps)]
-            s_im = [spec_second[v * replicas + k, :, im_at] for v in range(low, steps)]
-            for u in range(half, steps):
-                re, im = None, None
-                for v in range(low, u + 1):
-                    j, w = u - v, v - low
-                    re = add(re, h_re[j] * s_re[w] + h_im[j] * s_im[w])
-                    im = add(im, h_re2[j] * s_im[w] - h_im[j] * s_re[w])
-                prod[(u - half) * replicas + k, :, re_at] = re
-                prod[(u - half) * replicas + k, :, im_at] = im
-
-        def taps_products(c):
-            re_at, im_at, first = slices(c)
-            flip = jnp.where(first, 1.0, -turn)
-            sums_re, sums_im = [None] * count, [None] * count
-            for k in range(replicas):
-                t_re = [spec_first[steps + v * replicas + k, :, re_at] for v in range(half)]
-                t_im = [spec_first[steps + v * replicas + k, :, im_at] for v in range(half)]
-                for s in range(low, steps):
-                    s_re = spec_second[s * replicas + k, :, re_at]
-                    s_im = spec_second[s * replicas + k, :, im_at]
-                    s_re2 = jnp.where(first, s_im, s_re)
-                    s_im = jnp.where(first, 0.0, s_im)
-                    for v in range(max(s, half), steps):
-                        m, w = v - s, v - half
-                        sums_re[m] = add(sums_re[m], t_re[w] * s_re + t_im[w] * s_im)
-                        sums_im[m] = add(sums_im[m], t_im[w] * s_re2 - t_re[w] * s_im)
-            for m in range(count):
-                last = m == count - 1
-                tprod[m, :, re_at] = sums_re[m] if last else sums_re[m] + sign * sums_re[m + 1]
-                tprod[m, :, im_at] = flip * (sums_im[m] if last else sums_im[m] + sign * sums_im[m + 1])
-
-        def finish_second():
-            repeat(0, rows // lanes * replicas, second_products)
-            out_s[...] = inverse(prod, 0, members)
-            send_own(out_s, 0, 1, other)
-
-        def finish_taps():
-            repeat(0, rows // lanes, taps_products)
-            out_d[pl.ds(0, count)] = inverse(tprod, 0, count)
-            if low == 0:
-                arrived(part, d_recv_sem.at[1])
-                out_d[pl.ds(0, half)] = out_d[pl.ds(0, half)] + part[...]
-                d_each(lambda copy: copy.start(), True)
-            else:
-                part_copy().start()
-
         if low == 0:
+            finish_taps()
             finish_second()
-            finish_taps()
         else:
             finish_taps()
             finish_second()
@@ -586,7 +614,8 @@
     @pl.when(inner)
     def _():
         arrived(sig.at[0], out_send_sem.at[2])
-        d_each(lambda copy: copy.wait_send(), False)
+        d_each(0, lambda copy: copy.wait_send(), False)
+        d_each(half, lambda copy: copy.wait_send(), False)
 
     @pl.when(jnp.logical_not(inner))
     def _():

time: 31.7 us -> 30.3 us (0.956)
  Pallas kernels: 30.6 us -> 29.2 us
    pallas_call x1, Pallas kernels: 29.8 us -> 28.4 us  [fused(): pl.pallas_call(functools.partial(kernel, steps, replicas, replicas * inpu...]
where the time goes in v3:
time: 30.3 us; the launch traced here: 29.9 us
  Pallas kernels  29.2 us (96%)
  between operations  0.64 us (2%)
    pallas_call x1, Pallas kernels, fused(): pl.pallas_call(functools.partial(kernel, steps, replicas, replicas * inpu...  28.4 us
    pallas_call x1, Pallas kernels, fused(): pl.pallas_call(hand_over, out_shape=tuple((jax.ShapeDtypeStruct(part.shap...  0.83 us

profile of v3, /device:TPU:0, one launch (start us, length us, event | category | flops | bytes accessed | tf_op | source)
XLA Modules:
  0.0 29.9 jit_solution(9864280665109553293)
XLA Ops:
  0.6 28.4 %shard_map.112 = (f32[512,128]{1,0:T(8,128)S(1)}, f32[512,128]{1,0:T(8,128)S(1)}, f32[32,512]{1,0:T(8,128)S(1)}) custom-call(f32[512,128]{1,0:T(8,128)} %bitcast.7, f32[512,128]{1,0:T(8,128)} %bitcast.8, f32[512,128]{1,0:T(8,128)} %bitcast.9, f32[512,128]{1,0:T(8,128)} %taps_any.1, f32[1,128]{1,0:T(1,128)} %bitcast.10, ...), custom_call_target="tpu_custom_call" | custom-call | tf_op jit(solution)/shard_map/pallas_call | solution.py:650
  29.0 0.8 %shard_map.113 = (f32[512,128]{1,0:T(8,128)}, f32[512,128]{1,0:T(8,128)}, f32[32,512]{1,0:T(8,128)}) custom-call(f32[512,128]{1,0:T(8,128)S(1)} %get-tuple-element.9.refs_0_, f32[512,128]{1,0:T(8,128)S(1)} %get-tuple-element.10.refs_1_, f32[32,512]{1,0:T(8,128)S(1)} %get-tuple-element.11.refs_2_), custom_call_target="tpu_custom_call" | custom-call | tf_op jit(solution)/shard_map/pallas_call | solution.py:680

commit v4 on v3

--- a/solution.py
+++ b/solution.py
@@ -265,12 +265,12 @@
     def arrived(ref, sem):
         pltpu.make_async_copy(ref, ref, sem).wait()
 
-    def repeat(low, high, use):
+    def repeat(low, high, use, unroll=1):
         def body(i, carry):
             use(i)
             return carry
 
-        lax.fori_loop(low, high, body, 0)
+        lax.fori_loop(low, high, body, 0, unroll=unroll)
 
     def slot_of(block, of_side):
         return jnp.where(of_side == 0, steps - 1 - block, block)
@@ -476,7 +476,7 @@
                 prod[u * replicas + k, :, re_at] = re
                 prod[u * replicas + k, :, im_at] = im
 
-        repeat(0, rows // lanes * replicas, first_products)
+        repeat(0, rows // lanes * replicas, first_products, 4)
 
         def inverse(source, start, size):
             return dot3(
@@ -484,9 +484,10 @@
             ).reshape(size, 8, rows)
 
         if low == 0:
-            out_t[pl.ds(0, members)] = inverse(prod, 0, members)
+            out_t[...] = inverse(prod, 0, 2 * members)
             send_cross()
-        out_t[pl.ds(members, members)] = inverse(prod, members, members)
+        else:
+            out_t[pl.ds(members, members)] = inverse(prod, members, members)
         send_own(out_t, members, 0, side)
 
         def transform(start):
@@ -511,7 +512,7 @@
                     prod[at, :, re_at] = re
                     prod[at, :, im_at] = im
 
-            repeat(0, rows // lanes * replicas, body)
+            repeat(0, rows // lanes * replicas, body, 4)
 
         def taps_products(begin, end, extend):
             def body(c):
@@ -590,6 +591,9 @@
         else:
             gg_out[...] = og[...] * (positions(0) + gain * inp[...])
         late = 0 if is_second else 1
+        scale = 1.0 / math.sqrt(batch_total * rows * steps)
+        arrived(res_taps, d_recv_sem.at[0])
+        fg_out[...] = scale * res_taps[...].reshape(width // replicas, rows)
         arrived(res_cross, out_recv_sem.at[2])
         arrived(res.at[late], out_recv_sem.at[1])
         res[late, ranges] = res[late, ranges] + res_cross[...]
@@ -597,17 +601,19 @@
             gg_out[...] = og[...] * (positions(0) + gain * inp[...])
         else:
             ig_out[...] = positions(1) + gain * gate[...]
-        scale = 1.0 / math.sqrt(batch_total * rows * steps)
-        arrived(res_taps, d_recv_sem.at[0])
-        fg_out[...] = scale * res_taps[...].reshape(width // replicas, rows)
-
-    pl.when(side == 0)(lambda: finish(False))
-    pl.when(side == 1)(lambda: finish(True))
 
     h_each(lambda s: h_copy(s, s).wait_send(), None)
     arrived(sig.at[0, pl.ds(0, members - 1)], in_send_sem.at[0])
     arrived(sig.at[0, pl.ds(0, members - 1)], in_send_sem.at[1])
     arrived(sig.at[0, pl.ds(0, ahead)], in_send_sem.at[2])
+
+    @pl.when(inner)
+    def _():
+        d_each(half, lambda copy: copy.wait_send(), False)
+
+    pl.when(side == 0)(lambda: finish(False))
+    pl.when(side == 1)(lambda: finish(True))
+
     arrived(sig.at[0, pl.ds(0, members - 1)], out_send_sem.at[0])
     arrived(sig.at[0, pl.ds(0, members - 1)], out_send_sem.at[1])
 
@@ -615,7 +621,6 @@
     def _():
         arrived(sig.at[0], out_send_sem.at[2])
         d_each(0, lambda copy: copy.wait_send(), False)
-        d_each(half, lambda copy: copy.wait_send(), False)
 
     @pl.when(jnp.logical_not(inner))
     def _():

time: 30.3 us -> 29.9 us (0.987)
  no operation moved by 1% of the time
where the time goes in v4:
time: 29.9 us; the launch traced here: 29.6 us
  Pallas kernels  29 us (97%)
  between operations  0.64 us (2%)
    pallas_call x1, Pallas kernels, fused(): pl.pallas_call(functools.partial(kernel, steps, replicas, replicas * inpu...  28.1 us
    pallas_call x1, Pallas kernels, fused(): pl.pallas_call(hand_over, out_shape=tuple((jax.ShapeDtypeStruct(part.shap...  0.83 us

profile of v4, /device:TPU:0, one launch (start us, length us, event | category | flops | bytes accessed | tf_op | source)
XLA Modules:
  0.0 29.6 jit_solution(8327518482316239019)
XLA Ops:
  0.6 28.1 %shard_map.112 = (f32[512,128]{1,0:T(8,128)S(1)}, f32[512,128]{1,0:T(8,128)S(1)}, f32[32,512]{1,0:T(8,128)S(1)}) custom-call(f32[512,128]{1,0:T(8,128)} %bitcast.7, f32[512,128]{1,0:T(8,128)} %bitcast.8, f32[512,128]{1,0:T(8,128)} %bitcast.9, f32[512,128]{1,0:T(8,128)} %taps_any.1, f32[1,128]{1,0:T(1,128)} %bitcast.10, ...), custom_call_target="tpu_custom_call" | custom-call | tf_op jit(solution)/shard_map/pallas_call | solution.py:655
  28.8 0.8 %shard_map.113 = (f32[512,128]{1,0:T(8,128)}, f32[512,128]{1,0:T(8,128)}, f32[32,512]{1,0:T(8,128)}) custom-call(f32[512,128]{1,0:T(8,128)S(1)} %get-tuple-element.9.refs_0_, f32[512,128]{1,0:T(8,128)S(1)} %get-tuple-element.10.refs_1_, f32[32,512]{1,0:T(8,128)S(1)} %get-tuple-element.11.refs_2_), custom_call_target="tpu_custom_call" | custom-call | tf_op jit(solution)/shard_map/pallas_call | solution.py:685

commit v5 on v4

--- a/solution.py
+++ b/solution.py
@@ -254,7 +254,7 @@
     ]
     for copy in loads:
         copy.start()
-    lax.fori_loop(1, devices, greet, 0)
+    lax.fori_loop(1, devices, greet, 0, unroll=True)
 
     def remote(src, dst, src_sem, dst_sem, s, d):
         return pltpu.make_async_remote_copy(
@@ -312,7 +312,7 @@
                 half * side + q // replicas, lax.rem(q, replicas),
             ).start()
 
-        repeat(1, members, body)
+        repeat(1, members, body, 5)
         pltpu.make_async_copy(sig.at[which, group], dst_ref.at[base + own_row], in_recv_sem.at[kind]).start()
 
     def crossing():
@@ -324,7 +324,7 @@
                 half * other + q // replicas, lax.rem(q, replicas),
             ).start()
 
-        repeat(0, ahead, body)
+        repeat(0, ahead, body, 4)
 
     def prepare_input():
         loads[1].wait()
@@ -372,13 +372,13 @@
     def first_served(use):
         def body(i):
             q = lax.rem(place + i, members)
-            pl.when(jnp.logical_and(q >= 4, q != place))(lambda: use(q))
+            pl.when(jnp.logical_and(q >= 6, q != place))(lambda: use(q))
 
         def served(q):
             pl.when(q != place)(lambda: use(q))
 
-        repeat(0, 4, served)
-        repeat(1, members, body)
+        repeat(0, 6, served)
+        repeat(1, members, body, 5)
 
     def send_own(source, base, kind, which):
         def use(q):
@@ -401,8 +401,8 @@
                 s, lax.rem(q, replicas),
             ).start()
 
-        repeat(0, 4, use)
-        repeat(0, members, lambda i: pl.when(lax.rem(place + i, members) >= 4)(lambda: use(lax.rem(place + i, members))))
+        repeat(0, 6, use)
+        repeat(0, members, lambda i: pl.when(lax.rem(place + i, members) >= 6)(lambda: use(lax.rem(place + i, members))))
 
     d_dst = group // (members // replicas)
     d_at = lax.rem(group, members // replicas)

time: 29.9 us -> 29.9 us (level)
  Pallas kernels: 29 us -> 28.7 us
where the time goes in v5:
time: 29.9 us; the launch traced here: 29.3 us
  Pallas kernels  28.7 us (96%)
  between operations  0.64 us (2%)
    pallas_call x1, Pallas kernels, fused(): pl.pallas_call(functools.partial(kernel, steps, replicas, replicas * inpu...  27.9 us
    pallas_call x1, Pallas kernels, fused(): pl.pallas_call(hand_over, out_shape=tuple((jax.ShapeDtypeStruct(part.shap...  0.83 us

profile of v5, /device:TPU:0, one launch (start us, length us, event | category | flops | bytes accessed | tf_op | source)
XLA Modules:
  0.0 29.3 jit_solution(7599687435823993125)
XLA Ops:
  0.6 27.9 %shard_map.112 = (f32[512,128]{1,0:T(8,128)S(1)}, f32[512,128]{1,0:T(8,128)S(1)}, f32[32,512]{1,0:T(8,128)S(1)}) custom-call(f32[512,128]{1,0:T(8,128)} %bitcast.7, f32[512,128]{1,0:T(8,128)} %bitcast.8, f32[512,128]{1,0:T(8,128)} %bitcast.9, f32[512,128]{1,0:T(8,128)} %taps_any.1, f32[1,128]{1,0:T(1,128)} %bitcast.10, ...), custom_call_target="tpu_custom_call" | custom-call | tf_op jit(solution)/shard_map/pallas_call | solution.py:655
  28.5 0.8 %shard_map.113 = (f32[512,128]{1,0:T(8,128)}, f32[512,128]{1,0:T(8,128)}, f32[32,512]{1,0:T(8,128)}) custom-call(f32[512,128]{1,0:T(8,128)S(1)} %get-tuple-element.9.refs_0_, f32[512,128]{1,0:T(8,128)S(1)} %get-tuple-element.10.refs_1_, f32[32,512]{1,0:T(8,128)S(1)} %get-tuple-element.11.refs_2_), custom_call_target="tpu_custom_call" | custom-call | tf_op jit(solution)/shard_map/pallas_call | solution.py:685
